TPU v7x, 32 devices: a whole 2x2x4 slice. The times are simulated.
32 devices in a mesh: groups: 1, expert: 8 (over z, y), dp: 4 (over x, core).
Axes of the slice: x: 2, y: 2, z: 4, core: 2. Of those that a mesh axis runs over, the one named last changes fastest.
Arguments:
- tokens: bfloat16 [4096, 2048], P(('groups', 'expert', 'dp')), may hold values from -6 to 6
- expert_ids: int32 [4096, 8], P(('groups', 'expert', 'dp')), may hold values from 0 to 15, all different within a row; in each aligned block of 128 rows (0 to 127, 128 to 255, ...) at most 96 rows name the same one
- gate_scores: float32 [4096, 8], P(('groups', 'expert', 'dp')), may hold values from 0.05 to 1
- w_gate: bfloat16 [32, 2048, 192], P(('expert', 'dp')), may hold values from -0.125 to 0.125
- w_up: bfloat16 [32, 2048, 192], P(('expert', 'dp')), may hold values from -0.125 to 0.125
- w_down: bfloat16 [32, 192, 2048], P(('expert', 'dp')), may hold values from -0.3125 to 0.3125
- projector: bfloat16 [2048, 1536], P(None, 'dp'), may hold values from -0.125 to 0.125
- student: bfloat16 [4096, 1536], P(('groups', 'expert'), 'dp'), may hold values from -6 to 6
- target_mask: int32 [4096], P(('groups', 'expert')), may hold values 0 or 1
Outputs:
- projected: bfloat16 [4096, 1536], P(('groups', 'expert'), 'dp')
- proj_grad: float32 [2048, 1536], P(('groups', 'expert'), 'dp')
Inputs may be any that keep to these rules, and one draw needn't show every extreme that they name: `expert_ids`: each token names 8 different experts. Within each aligned block of 128 tokens (the tokens of one device) no expert is named by more than 96 tokens, and in every draw some expert is named by exactly 96 tokens of some block.
All inputs are finite; a program needn't handle non-finite values. No bound on the sum of `target_mask` on one device may be relied on, other than what follows from the above.
Results may differ from a plain program's by a relative error of at most 0.012.
Values may be sent and summed in bfloat16 or wider, within the bound.
A program may use at most 128 MiB of HBM per device.

v0:
```python
import math

import jax
import jax.numpy as jnp
from jax import lax
from jax.sharding import PartitionSpec as P


def from_partner(block, axis, apart):
    count = lax.axis_size(axis)
    route = []
    for low in range(count):
        high = low | 1 << apart
        if high != low and high < count:
            route += [(low, high), (high, low)]
    return lax.ppermute(block, axis, route)


def half_hidden(slot_rows, gate_half, up_half):
    gate_pre = jnp.dot(slot_rows, gate_half, preferred_element_type=jnp.float32)
    up_pre = jnp.dot(slot_rows, up_half, preferred_element_type=jnp.float32)
    return (jax.nn.silu(gate_pre) * up_pre).astype(jnp.bfloat16)


def body(tokens, expert_ids, gate_scores, w_gate, w_up, w_down, projector, student, target_mask):
    tok_count = tokens.shape[0]
    model_width = tokens.shape[1]
    top_count = expert_ids.shape[1]
    expert_axis = lax.axis_size("expert")
    data_axis = lax.axis_size("dp")
    expert_total = expert_axis * data_axis // 2
    capacity = min(
        tok_count, 2 * ((3 * tok_count * top_count + 4 * expert_total - 1) // (4 * expert_total))
    )
    half_cap = capacity // 2
    slot_total = expert_total * capacity
    expert_iota = jnp.arange(expert_total, dtype=jnp.int32)
    naming = (expert_ids[:, :, None] == expert_iota[None, None, :]).astype(jnp.int32)
    expert_hits = jnp.sum(naming, axis=1)
    earlier = jnp.cumsum(expert_hits, axis=0) - expert_hits
    slot_index = jnp.sum(naming * earlier[:, None, :], axis=2)
    position = expert_ids * capacity + slot_index
    token_iota = jnp.broadcast_to(
        jnp.arange(tok_count, dtype=jnp.int32)[:, None], (tok_count, top_count)
    )
    slot_table = (
        jnp.full((slot_total,), tok_count, jnp.int32)
        .at[position.reshape(-1)]
        .set(token_iota.reshape(-1))
    )
    padded_tokens = jnp.concatenate([tokens, jnp.zeros((1, model_width), tokens.dtype)], axis=0)
    send_rows = jnp.take(padded_tokens, slot_table, axis=0)
    send_rows = send_rows.reshape(expert_axis, data_axis, half_cap, model_width)
    arrived = lax.all_to_all(
        lax.all_to_all(send_rows, "expert", split_axis=0, concat_axis=0, tiled=True),
        "dp",
        split_axis=1,
        concat_axis=1,
        tiled=True,
    )
    slot_rows = arrived.reshape(slot_total, model_width)
    gate_mine = w_gate[0]
    up_mine = w_up[0]
    down_mine = w_down[0]
    gate_other, up_other, down_other = from_partner((gate_mine, up_mine, down_mine), "dp", 0)
    hidden_mine = half_hidden(slot_rows, gate_mine, up_mine)
    hidden_other = half_hidden(slot_rows, gate_other, up_other)
    expert_out = (
        jnp.dot(hidden_mine, down_mine, preferred_element_type=jnp.float32)
        + jnp.dot(hidden_other, down_other, preferred_element_type=jnp.float32)
    ).astype(jnp.bfloat16)
    came_back = lax.all_to_all(
        lax.all_to_all(
            expert_out.reshape(expert_axis, data_axis, half_cap, model_width),
            "expert",
            split_axis=0,
            concat_axis=0,
            tiled=True,
        ),
        "dp",
        split_axis=1,
        concat_axis=1,
        tiled=True,
    )
    returned = came_back.reshape(slot_total, model_width)
    norm_gates = gate_scores / jnp.sum(gate_scores, axis=1, keepdims=True)
    combined = jnp.zeros((tok_count, model_width), jnp.float32)
    for column in range(top_count):
        picked = jnp.take(returned, position[:, column], axis=0)
        combined = combined + norm_gates[:, column : column + 1] * picked.astype(jnp.float32)
    teacher_out = combined.astype(jnp.bfloat16)
    grad_scale = 1.0 / math.sqrt(tok_count * expert_axis * data_axis)
    mask_rows = target_mask.astype(jnp.float32)
    portion = lax.all_gather(teacher_out, "dp", axis=0, tiled=True)
    proj_part = jnp.dot(portion, projector, preferred_element_type=jnp.float32)
    target_part = student.astype(jnp.float32)
    error_part = (mask_rows[:, None] * (proj_part - target_part)).astype(jnp.bfloat16)
    grad_term = lax.dot_general(
        portion, error_part, (((0,), (0,)), ((), ())), preferred_element_type=jnp.float32
    )
    projected_all = proj_part
    projected_all, grad_term = (projected_all, grad_term)
    grad_part = (
        lax.psum_scatter(
            grad_term.astype(jnp.bfloat16), "expert", scatter_dimension=0, tiled=True
        ).astype(jnp.float32)
        * grad_scale
    )
    return (projected_all.astype(jnp.bfloat16), grad_part)


def solution(mesh):
    return jax.shard_map(
        body,
        mesh=mesh,
        in_specs=(
            P(("groups", "expert", "dp"), None),
            P(("groups", "expert", "dp"), None),
            P(("groups", "expert", "dp"), None),
            P(("expert", "dp"), None, None),
            P(("expert", "dp"), None, None),
            P(("expert", "dp"), None, None),
            P(None, "dp"),
            P(("groups", "expert"), "dp"),
            P(("groups", "expert")),
        ),
        out_specs=(P(("groups", "expert"), "dp"), P(("groups", "expert"), "dp")),
        check_vma=False,
    )
```

profile of v0, /device:TPU:0, one launch (start us, length us, event | category | flops | bytes accessed | tf_op | source)
XLA Modules:
  0.0 663.7 jit_solution(9635469128757528363)
XLA Ops:
  7.2 0.8 convert_reduce_fusion
  8.0 0.1 copy.32
  8.1 0.2 reduce_window_sum.11
  8.3 0.1 copy.34
  8.3 0.7 select_reduce_fusion
  9.1 0.7 multiply_add_fusion
  9.8 0.1 copy.35
  9.9 0.1 reshape.76
  10.0 0.1 reshape.157
  10.1 4.3 scatter_custom_fusion
  14.4 0.1 broadcast_in_dim.41
  14.5 1.1 concatenate.3
  15.6 7.1 %gather_fusion = bf16[1536,2048]{1,0:T(8,128)(2,1)} fusion(bf16[129,2048]{1,0:T(8,128)(2,1)S(1)} %concatenate.3, s32[2048]{0:T(1024)S(1)} %pad_clamp_fusion), kind=kCustom, calls=%fused_computation.8 | custom fusion | bytes 12589056 | tf_op jit(solution)/shard_map/jit(_take)/gather | solution.py:52
  22.7 3.4 broadcast_select_fusion
  26.1 145.2 %all_to_all.20 = bf16[8,4,48,2048]{3,2,1,0:T(8,128)(2,1)S(1)} all-to-all(bf16[8,4,48,2048]{3,2,1,0:T(8,128)(2,1)S(1)} %broadcast_select_fusion), channel_id=1, replica_groups=mesh['groups'=1,'expert'=8,'dp'=4] {'expert'}, dimensions={0} | all-to-all | bytes 12582912 | tf_op jit(solution)/shard_map/all_to_all | solution.py:55
  171.3 3.2 copy.36
  174.6 5.5 all-to-all-start.1
  180.1 0.3 collective-permute-start
  180.4 0.3 collective-permute-start.1
  180.7 0.2 collective-permute-start.2
  180.9 69.7 %all-to-all-done.1 = bf16[8,4,48,2048]{3,2,0,1:T(8,128)(2,1)} async-done(((bf16[8,4,48,2048]{3,2,0,1:T(8,128)(2,1)}), bf16[8,4,48,2048]{3,2,0,1:T(8,128)(2,1)}, u32[]{:S(2)}, u32[]{:S(2)}) %all-to-all-start.1) | async-done | bytes 6291488 | tf_op jit(solution)/shard_map/all_to_all | solution.py:54
  250.6 3.4 copy.37
  254.0 3.2 fusion.15
  257.2 3.3 fusion.22
  260.6 11.7 %fusion.1 = f32[1536,2048]{1,0:T(8,128)} fusion(bf16[1536,2048]{1,0:T(8,128)(2,1)} %bitcast.75, f32[1536,192]{0,1:T(8,128)} %fusion.15, bf16[1,192,2048]{2,1,0:T(8,128)(2,1)} %param.16, bf16[1,2048,192]{1,2,0:T(8,128)(2,1)S(1)} %copy-done.2), kind=kOutput, calls=%fused_computation.15 | convolution fusion | flops 2417688576 | bytes 21626880 | tf_op jit(solution)/shard_map/dot_general | solution.py:69
  272.3 13.4 %add_convert_fusion = bf16[1536,2048]{1,0:T(8,128)(2,1)} fusion(f32[1536,2048]{1,0:T(8,128)} %fusion.1, bf16[192,2048]{1,0:T(8,128)(2,1)} %collective-permute-done.2, f32[1536,192]{0,1:T(8,128)S(1)} %fusion.22, bf16[1536,2048]{1,0:T(8,128)(2,1)} %bitcast.76, bf16[2048,192]{0,1:T(8,128)(2,1)} %collective-permute-done.1), kind=kOutput, calls=%fused_computation.10 | convolution fusion | flops 2423980032 | bytes 27918336 | tf_op jit(solution)/shard_map/dot_general | solution.py:70
  285.7 141.9 %all_to_all.21 = bf16[8,4,48,2048]{3,2,1,0:T(8,128)(2,1)S(1)} all-to-all(bf16[8,4,48,2048]{3,2,1,0:T(8,128)(2,1)} %bitcast.77), channel_id=1, replica_groups=mesh['groups'=1,'expert'=8,'dp'=4] {'expert'}, dimensions={0} | all-to-all | bytes 12582912 | tf_op jit(solution)/shard_map/all_to_all | solution.py:73
  427.6 3.2 copy.38
  430.9 5.4 all-to-all-start.3
  436.2 0.3 all-gather.2.cloned.1.call-start
  436.6 70.3 %all-to-all-done.3 = bf16[8,4,48,2048]{3,2,0,1:T(8,128)(2,1)} async-done(((bf16[8,4,48,2048]{3,2,0,1:T(8,128)(2,1)}), bf16[8,4,48,2048]{3,2,0,1:T(8,128)(2,1)}, u32[]{:S(2)}, u32[]{:S(2)}) %all-to-all-start.3) | async-done | bytes 6291488 | tf_op jit(solution)/shard_map/all_to_all | solution.py:72
  506.9 6.6 copy.39
  513.5 5.0 gather_fusion.2
  518.5 5.0 gather_fusion.3
  523.6 5.0 gather_fusion.4
  528.6 5.8 gather_fusion.5
  534.4 5.8 gather_fusion.6
  540.3 5.9 gather_fusion.1
  546.2 6.1 gather_fusion.7
  552.3 5.9 gather_fusion.8
  558.2 3.3 add_convert_fusion.1
  561.5 0.0 all-gather.2.cloned.1.call-update
  561.5 0.0 reduce-scatter.2.cloned.1.call-start
  561.6 20.7 %all-gather.2.cloned.1.call-done = bf16[512,2048]{1,0:T(8,128)(2,1)} async-done(((bf16[128,2048]{1,0:T(8,128)(2,1)}), bf16[512,2048]{1,0:T(8,128)(2,1)}) %all-gather.2.cloned.1.call-update) | async-done | bytes 2097168 | tf_op jit(solution)/shard_map/all_gather | solution.py:94
  582.3 3.6 fusion.19
  585.9 4.2 convolution_convert_fusion
  590.1 65.1 %reduce-scatter.2.cloned.1.call-done = bf16[256,384]{1,0:T(8,128)(2,1)} async-done(((bf16[2048,384]{1,0:T(8,128)(2,1)}), bf16[256,384]{1,0:T(8,128)(2,1)}) %reduce-scatter.2.cloned.1.call-update) | async-done | bytes 196624 | tf_op jit(solution)/shard_map/reduce_scatter | solution.py:104
  655.2 1.7 convert_multiply_fusion
  (31 shorter events, 0.2 us)
Async XLA Ops:
  7.2 575.2 %copy-start = (bf16[2048,384]{1,0:T(8,128)(2,1)S(1)}, bf16[2048,384]{1,0:T(8,128)(2,1)}, u32[]{:S(2)}) copy-start(bf16[2048,384]{1,0:T(8,128)(2,1)} %param.17) | copy-start | bytes 4718596
  174.6 5.6 copy-start.5
  174.6 5.8 copy-start.2
  174.6 76.1 %all-to-all-start.1 = ((bf16[8,4,48,2048]{3,2,0,1:T(8,128)(2,1)}), bf16[8,4,48,2048]{3,2,0,1:T(8,128)(2,1)}, u32[]{:S(2)}, u32[]{:S(2)}) async-start(bf16[8,4,48,2048]{3,2,0,1:T(8,128)(2,1)} %copy.36), calls=%async_computation.1 | async-start | bytes 12582912 | tf_op jit(solution)/shard_map/all_to_all | solution.py:54
  180.1 77.1 %collective-permute-start = (bf16[2048,192]{0,1:T(8,128)(2,1)S(1)}, bf16[2048,192]{0,1:T(8,128)(2,1)}, u32[]{:S(2)}, u32[]{:S(2)}) collective-permute-start(bf16[2048,192]{0,1:T(8,128)(2,1)S(1)} %bitcast.81), channel_id=1, source_target_pairs={{0,1},{1,0},{2,3},{3,2},{4,5},{5,4},{6,7},{7,6},{8,9},{9,8},{10,11... | collective-permute-start | bytes 2359304 | tf_op jit(solution)/shard_map/ppermute | solution.py:16
  180.4 91.9 %collective-permute-start.1 = (bf16[2048,192]{0,1:T(8,128)(2,1)S(1)}, bf16[2048,192]{0,1:T(8,128)(2,1)}, u32[]{:S(2)}, u32[]{:S(2)}) collective-permute-start(bf16[2048,192]{0,1:T(8,128)(2,1)S(1)} %bitcast.79), channel_id=1, source_target_pairs={{0,1},{1,0},{2,3},{3,2},{4,5},{5,4},{6,7},{7,6},{8,9},{9,8},{10,11... | collective-permute-start | bytes 2359304 | tf_op jit(solution)/shard_map/ppermute | solution.py:16
  180.7 91.6 %collective-permute-start.2 = (bf16[192,2048]{1,0:T(8,128)(2,1)}, bf16[192,2048]{1,0:T(8,128)(2,1)}, u32[]{:S(2)}, u32[]{:S(2)}) collective-permute-start(bf16[192,2048]{1,0:T(8,128)(2,1)} %bitcast.7), channel_id=1, source_target_pairs={{0,1},{1,0},{2,3},{3,2},{4,5},{5,4},{6,7},{7,6},{8,9},{9,8},{10,11... | collective-permute-start | bytes 2359304 | tf_op jit(solution)/shard_map/ppermute | solution.py:16
  254.0 3.2 copy-start.1
  430.8 5.6 copy-start.3
  430.9 76.1 %all-to-all-start.3 = ((bf16[8,4,48,2048]{3,2,0,1:T(8,128)(2,1)}), bf16[8,4,48,2048]{3,2,0,1:T(8,128)(2,1)}, u32[]{:S(2)}, u32[]{:S(2)}) async-start(bf16[8,4,48,2048]{3,2,0,1:T(8,128)(2,1)} %copy.38), calls=%async_computation.3 | async-start | bytes 12582912 | tf_op jit(solution)/shard_map/all_to_all | solution.py:72
  436.2 146.1 %all-gather.2.cloned.1.call-start = ((), (), s32[]{:S(2)}) async-start(), calls=%async_computation.5 | async-start | bytes 2621440 | tf_op jit(solution)/shard_map/all_gather | solution.py:94
  546.2 15.4 %copy-start.4 = (s32[512]{0:T(512)S(1)}, s32[512]{0:T(512)}, u32[]{:S(2)}) copy-start(s32[512]{0:T(512)} %param.19) | copy-start | bytes 6148
  561.5 93.6 %reduce-scatter.2.cloned.1.call-start = ((), (), s32[]{:S(2)}) async-start(), calls=%async_computation.6 | async-start | bytes 1769472 | tf_op jit(solution)/shard_map/reduce_scatter | solution.py:104
Sparse Core Ops, SparseCore 0:
  561.6 20.6 all-gather.1
  590.2 64.9 reduce-scatter.1
where the time goes:
time: 665 us; the launch traced here: 664 us
  blocking collectives  287 us (43%)
  waiting for transfers between devices  226 us (34%)
  local copies, waits for them, and re-layouts  74.1 us (11%)
  matrix products  39.4 us (6%)
  between operations  14.3 us (2%)
  starting transfers between devices  12 us (2%)
  other arithmetic  11 us (2%)
    all_to_all x1, blocking collectives, body(): lax.all_to_all(send_rows, 'expert', split_axis=0, concat_axis=0, tiled=True)  145 us
    all_to_all x1, blocking collectives, body(): lax.all_to_all(expert_out.reshape(expert_axis, data_axis, half_cap, model...  142 us
    all_to_all x1, waiting for transfers between devices, body(): lax.all_to_all(lax.all_to_all(expert_out.reshape(expert_axis, data_axis,...  70.3 us
    all_to_all x1, waiting for transfers between devices, body(): lax.all_to_all(lax.all_to_all(send_rows, 'expert', split_axis=0, concat_a...  69.7 us
    reduce_scatter x1, waiting for transfers between devices, body(): lax.psum_scatter(grad_term.astype(jnp.bfloat16), 'expert', scatter_dimens...  65.1 us
    gather x8, local copies, waits for them, and re-layouts, body(): picked = jnp.take(returned, position[:, column], axis=0)  44.6 us
    all_gather x1, waiting for transfers between devices, body(): portion = lax.all_gather(teacher_out, 'dp', axis=0, tiled=True)  20.7 us
    dot_general x1, matrix products, body(): jnp.dot(hidden_other, down_other, preferred_element_type=jnp.float32)  13.4 us
  transfers between devices with their start and end apart: 7, of which 4 were waited for; matrix products, arithmetic and copies ran while one was open for 3% of the time, Pallas kernels for 0%

commit v1 on v0

--- a/solution.py
+++ b/solution.py
@@ -22,7 +22,7 @@
     return (jax.nn.silu(gate_pre) * up_pre).astype(jnp.bfloat16)
 
 
-def body(tokens, expert_ids, gate_scores, w_gate, w_up, w_down, projector, student, target_mask):
+def routed_body(tokens, expert_ids, gate_scores, w_gate, w_up, w_down, projector, student, target_mask):
     tok_count = tokens.shape[0]
     model_width = tokens.shape[1]
     top_count = expert_ids.shape[1]
@@ -89,7 +89,43 @@
         picked = jnp.take(returned, position[:, column], axis=0)
         combined = combined + norm_gates[:, column : column + 1] * picked.astype(jnp.float32)
     teacher_out = combined.astype(jnp.bfloat16)
-    grad_scale = 1.0 / math.sqrt(tok_count * expert_axis * data_axis)
+    return finish(teacher_out, projector, student, target_mask)
+
+
+def dense_body(tokens, expert_ids, gate_scores, w_gate, w_up, w_down, projector, student, target_mask):
+    tok_count, model_width = tokens.shape
+    expert_axis = lax.axis_size("expert")
+    data_axis = lax.axis_size("dp")
+    expert_total = expert_axis * data_axis // 2
+    held = data_axis // 2
+    norm_gates = gate_scores / jnp.sum(gate_scores, axis=1, keepdims=True)
+    iota = jnp.arange(expert_total, dtype=jnp.int32)
+    dense_gates = jnp.sum(
+        jnp.where(expert_ids[:, :, None] == iota[None, None, :], norm_gates[:, :, None], 0.0), axis=1
+    )
+    all_tokens = lax.all_gather(tokens, "expert", axis=0, tiled=True)
+    all_gates = lax.all_gather(dense_gates, "expert", axis=0, tiled=True)
+    gate_all = lax.all_gather(w_gate, "dp", axis=0, tiled=True)
+    up_all = lax.all_gather(w_up, "dp", axis=0, tiled=True)
+    down_all = lax.all_gather(w_down, "dp", axis=0, tiled=True)
+    mine = lax.axis_index("expert") * held
+    summed = jnp.zeros((tok_count * expert_axis, model_width), jnp.float32)
+    for local in range(held):
+        out = jnp.zeros((tok_count * expert_axis, model_width), jnp.float32)
+        for half in range(2):
+            slab = 2 * local + half
+            hidden = half_hidden(all_tokens, gate_all[slab], up_all[slab])
+            out = out + jnp.dot(hidden, down_all[slab], preferred_element_type=jnp.float32)
+        gate = lax.dynamic_slice_in_dim(all_gates, mine + local, 1, axis=1)
+        summed = summed + gate * out.astype(jnp.bfloat16).astype(jnp.float32)
+    teacher_out = lax.psum_scatter(
+        summed.astype(jnp.bfloat16), "expert", scatter_dimension=0, tiled=True
+    )
+    return finish(teacher_out, projector, student, target_mask)
+
+
+def finish(teacher_out, projector, student, target_mask):
+    grad_scale = 1.0 / math.sqrt(teacher_out.shape[0] * lax.axis_size("expert") * lax.axis_size("dp"))
     mask_rows = target_mask.astype(jnp.float32)
     portion = lax.all_gather(teacher_out, "dp", axis=0, tiled=True)
     proj_part = jnp.dot(portion, projector, preferred_element_type=jnp.float32)
@@ -98,18 +134,18 @@
     grad_term = lax.dot_general(
         portion, error_part, (((0,), (0,)), ((), ())), preferred_element_type=jnp.float32
     )
-    projected_all = proj_part
-    projected_all, grad_term = (projected_all, grad_term)
     grad_part = (
         lax.psum_scatter(
             grad_term.astype(jnp.bfloat16), "expert", scatter_dimension=0, tiled=True
         ).astype(jnp.float32)
         * grad_scale
     )
-    return (projected_all.astype(jnp.bfloat16), grad_part)
+    return (proj_part.astype(jnp.bfloat16), grad_part)
 
 
 def solution(mesh):
+    experts = mesh.shape["expert"] * mesh.shape["dp"] // 2
+    body = dense_body if experts <= 32 else routed_body
     return jax.shard_map(
         body,
         mesh=mesh,

time: 665 us -> 406 us (0.61)
  blocking collectives: 287 us -> 32.3 us
  local copies, waits for them, and re-layouts: 74.1 us -> 0.61 us
  waiting for transfers between devices: 226 us -> 299 us
  matrix products: 39.4 us -> 55.9 us
  starting transfers between devices: 12 us -> 0.27 us
  other arithmetic: 11 us -> 3.8 us
    all_to_all x2 -> x0, blocking collectives: 287 us -> none  [the longest x1 145 us: body(): lax.all_to_all(send_rows, 'expert', split_axis=0, concat_axis=0, tiled=True)]
    all_to_all x2 -> x0, waiting for transfers between devices: 140 us -> none  [the longest x1 70.3 us: body(): lax.all_to_all(lax.all_to_all(expert_out.reshape(expert_axis, data_axis,...]
    all_gather x1 -> x5, waiting for transfers between devices: 20.7 us -> 143 us  [the longest x1 71.9 us: dense_body(): all_tokens = lax.all_gather(tokens, 'expert', axis=0, tiled=True)]
    reduce_scatter x1 -> x2, waiting for transfers between devices: 65.1 us -> 153 us  [the longest x1 88 us: dense_body(): lax.psum_scatter(summed.astype(jnp.bfloat16), 'expert', scatter_dimension...]
    gather x9 -> x0, local copies, waits for them, and re-layouts: 51.7 us -> none  [the longest x8 44.6 us: body(): picked = jnp.take(returned, position[:, column], axis=0)]
    all_gather x0 -> x1, blocking collectives: none -> 32.3 us  [dense_body(): all_gates = lax.all_gather(dense_gates, 'expert', axis=0, tiled=True)]
    all_to_all x4 -> x0, local copies, waits for them, and re-layouts: 16.4 us -> none  [the longest x1 6.58 us: body(): lax.all_to_all(lax.all_to_all(expert_out.reshape(expert_axis, data_axis,...]
    dot_general x4 -> x6, matrix products: 32.9 us -> 45.5 us  [the longest x4 39.2 us: dense_body(): jnp.dot(hidden, down_all[slab], preferred_element_type=jnp.float32)]
  transfers between devices with their start and end apart: 7 -> 7, of which waited for: 4 -> 6; matrix products, arithmetic and copies ran while one was open for 3% -> 3% of each run, Pallas kernels for 0% -> 0%
where the time goes in v1:
time: 406 us
  waiting for transfers between devices  299 us (74%)
  matrix products  55.9 us (14%)
  blocking collectives  32.3 us (8%)
  between operations  14.2 us (3%)
    reduce_scatter x1, waiting for transfers between devices, dense_body(): lax.psum_scatter(summed.astype(jnp.bfloat16), 'expert', scatter_dimension...  88 us
    all_gather x1, waiting for transfers between devices, dense_body(): all_tokens = lax.all_gather(tokens, 'expert', axis=0, tiled=True)  71.9 us
    reduce_scatter x1, waiting for transfers between devices, finish(): lax.psum_scatter(grad_term.astype(jnp.bfloat16), 'expert', scatter_dimens...  65 us
    dot_general x4, matrix products, dense_body(): jnp.dot(hidden, down_all[slab], preferred_element_type=jnp.float32)  39.2 us
    all_gather x1, blocking collectives, dense_body(): all_gates = lax.all_gather(dense_gates, 'expert', axis=0, tiled=True)  32.3 us
    all_gather x1, waiting for transfers between devices, dense_body(): down_all = lax.all_gather(w_down, 'dp', axis=0, tiled=True)  30 us
    all_gather x1, waiting for transfers between devices, finish(): portion = lax.all_gather(teacher_out, 'dp', axis=0, tiled=True)  23.8 us
    all_gather x1, waiting for transfers between devices, dense_body(): up_all = lax.all_gather(w_up, 'dp', axis=0, tiled=True)  17.3 us
  transfers between devices with their start and end apart: 7, of which 6 were waited for; matrix products, arithmetic and copies ran while one was open for 3% of the time, Pallas kernels for 0%

profile of v1, /device:TPU:0, one launch (start us, length us, event | category | flops | bytes accessed | tf_op | source)
XLA Modules:
  0.0 405.8 jit_solution(5051488343915732760)
XLA Ops:
  7.2 0.0 copy-start
  7.2 0.0 all-gather.8.cloned.1.call-start
  7.2 0.7 all-gather.8.cloned.1.call-update
  7.9 0.0 all-gather.6.cloned.1.call-start
  8.0 0.7 all-gather.6.cloned.1.call-update
  8.7 0.0 all-gather.10.cloned.1.call-start
  8.7 0.7 all-gather.10.cloned.1.call-update
  9.4 0.0 all-gather.12.cloned.1.call-start
  9.4 0.5 all-gather.12.cloned.1.call-update
  10.0 0.0 reduce-scatter.3.cloned.1.call-start
  10.0 0.7 reduce_sum.18
  10.7 0.7 broadcast_divide_fusion
  11.4 0.7 select_reduce_fusion
  12.1 32.3 %all_gather.18 = f32[1024,16]{0,1:T(8,128)S(1)} all-gather(f32[128,16]{0,1:T(8,128)S(1)} %select_reduce_fusion), channel_id=1, replica_groups=mesh['groups'=1,'expert'=8,'dp'=4] {'expert'}, dimensions={0}, use_global_device_ids=true | all-gather | bytes 73728 | tf_op jit(solution)/shard_map/all_gather | solution.py:107
  44.4 0.0 all-gather.8.cloned.1.call-done
  44.5 71.9 %all-gather.6.cloned.1.call-done = bf16[1024,2048]{1,0:T(8,128)(2,1)} async-done(((bf16[128,2048]{1,0:T(8,128)(2,1)}), bf16[1024,2048]{1,0:T(8,128)(2,1)}) %all-gather.6.cloned.1.call-update) | async-done | bytes 4194320 | tf_op jit(solution)/shard_map/all_gather | solution.py:106
  116.4 0.0 copy-start.1
  116.4 0.0 copy-start.3
  116.4 4.1 %fusion.7 = f32[1024,192]{0,1:T(8,128)S(1)} fusion(bf16[1024,2048]{1,0:T(8,128)(2,1)} %all-gather.6.cloned.1.call-done, bf16[4,2048,192]{1,2,0:T(8,128)(2,1)} %all-gather.8.cloned.1.call-done), kind=kOutput, calls=%fused_computation.21 | convolution fusion | flops 805306368 | bytes 5767168 | tf_op jit(solution)/shard_map/dot_general | solution.py:20
  120.5 0.0 copy-done.1
  120.5 0.6 copy-done.3
  121.1 1.5 fusion.6
  122.6 2.4 fusion.9
  125.0 2.4 fusion.8
  127.5 17.3 %all-gather.10.cloned.1.call-done = bf16[4,2048,192]{1,2,0:T(8,128)(2,1)} async-done(((bf16[1,2048,192]{1,2,0:T(8,128)(2,1)}), bf16[4,2048,192]{1,2,0:T(8,128)(2,1)}) %all-gather.10.cloned.1.call-update) | async-done | bytes 3145744 | tf_op jit(solution)/shard_map/all_gather | solution.py:109
  144.8 30.0 %all-gather.12.cloned.1.call-done = bf16[4,192,2048]{2,1,0:T(8,128)(2,1)} async-done(((bf16[1,192,2048]{2,1,0:T(8,128)(2,1)}), bf16[4,192,2048]{2,1,0:T(8,128)(2,1)}) %all-gather.12.cloned.1.call-update) | async-done | bytes 3145744 | tf_op jit(solution)/shard_map/all_gather | solution.py:110
  174.8 8.6 %fusion.4 = f32[1024,2048]{1,0:T(8,128)} fusion(bf16[1024,2048]{1,0:T(8,128)(2,1)} %all-gather.6.cloned.1.call-done, bf16[4,192,2048]{2,1,0:T(8,128)(2,1)} %all-gather.12.cloned.1.call-done, bf16[4,2048,192]{1,2,0:T(8,128)(2,1)} %all-gather.10.cloned.1.call-done, f32[1024,192]{0,1:T(8,128)S(1)} %fusion.7), kind=kOutput, calls=%fused_computation.12 | convolution fusion | flops 1611792384 | bytes 14942208 | tf_op jit(solution)/shard_map/dot_general | solution.py:118
  183.3 8.8 %fusion.1 = f32[1024,2048]{1,0:T(8,128)} fusion(bf16[1024,2048]{1,0:T(8,128)(2,1)} %all-gather.6.cloned.1.call-done, bf16[4,192,2048]{2,1,0:T(8,128)(2,1)} %all-gather.12.cloned.1.call-done, bf16[4,2048,192]{1,2,0:T(8,128)(2,1)} %all-gather.10.cloned.1.call-done, f32[1024,192]{0,1:T(8,128)} %fusion.9), kind=kOutput, calls=%fused_computation.9 | convolution fusion | flops 1611792384 | bytes 14942208 | tf_op jit(solution)/shard_map/dot_general | solution.py:118
  192.2 0.0 copy-start.6
  192.2 9.9 %add_convert_fusion.1 = bf16[1024,2048]{1,0:T(8,128)(2,1)} fusion(f32[1024,2048]{1,0:T(8,128)} %fusion.4, bf16[4,192,2048]{2,1,0:T(8,128)(2,1)} %all-gather.12.cloned.1.call-done, bf16[1024,2048]{1,0:T(8,128)(2,1)} %all-gather.6.cloned.1.call-done, bf16[4,2048,192]{1,2,0:T(8,128)(2,1)} %all-gather.10.cloned.1.call-done, f32[1024,192]{0,1:T(8,128)S(1)} %fusion.6), kind=kOutput, calls=%fused_computation.1 | convolution fusion | flops 1615986688 | bytes 19136512 | tf_op jit(solution)/shard_map/dot_general | solution.py:118
  202.1 0.0 copy-done.6
  202.1 11.9 %add_convert_fusion = bf16[1024,2048]{1,0:T(8,128)(2,1)} fusion(bf16[1024,2048]{1,0:T(8,128)(2,1)} %add_convert_fusion.1, f32[1024]{0:T(1024)S(1)} %bitcast.55, f32[1024]{0:T(1024)S(1)} %bitcast.54, f32[1024,2048]{1,0:T(8,128)} %fusion.1, bf16[4,192,2048]{2,1,0:T(8,128)(2,1)} %all-gather.12.cloned.1.call-done, ...), kind=kOutput, calls=%fused_computation | convolution fusion | flops 1628569600 | bytes 23339008 | tf_op jit(solution)/shard_map/dot_general | solution.py:118
  213.9 0.0 copy-start.2
  214.0 0.0 reduce-scatter.3.cloned.1.call-update
  214.0 0.0 all-gather.14.cloned.1.call-start
  214.0 88.0 %reduce-scatter.3.cloned.1.call-done = bf16[128,2048]{1,0:T(8,128)(2,1)} async-done(((bf16[1024,2048]{1,0:T(8,128)(2,1)}), bf16[128,2048]{1,0:T(8,128)(2,1)}) %reduce-scatter.3.cloned.1.call-update) | async-done | bytes 524304 | tf_op jit(solution)/shard_map/reduce_scatter | solution.py:121
  302.0 0.0 all-gather.14.cloned.1.call-update
  302.1 0.0 reduce-scatter.5.cloned.1.call-start
  302.1 0.0 copy-done.2
  302.1 23.8 %all-gather.14.cloned.1.call-done = bf16[512,2048]{1,0:T(8,128)(2,1)} async-done(((bf16[128,2048]{1,0:T(8,128)(2,1)}), bf16[512,2048]{1,0:T(8,128)(2,1)}) %all-gather.14.cloned.1.call-update) | async-done | bytes 2097168 | tf_op jit(solution)/shard_map/all_gather | solution.py:130
  325.9 0.0 copy-done
  325.9 3.7 fusion.34
  329.7 0.0 copy-done.5
  329.7 0.0 copy-done.4
  329.7 2.6 convolution_convert_fusion
  332.2 0.0 reduce-scatter.5.cloned.1.call-update
  332.2 65.0 %reduce-scatter.5.cloned.1.call-done = bf16[256,384]{1,0:T(8,128)(2,1)} async-done(((bf16[2048,384]{1,0:T(8,128)(2,1)}), bf16[256,384]{1,0:T(8,128)(2,1)}) %reduce-scatter.5.cloned.1.call-update) | async-done | bytes 196624 | tf_op jit(solution)/shard_map/reduce_scatter | solution.py:138
  397.2 1.7 convert_multiply_fusion
  (4 shorter events, 0.0 us)
Async XLA Ops:
  7.2 318.7 %copy-start = (bf16[2048,384]{1,0:T(8,128)(2,1)S(1)}, bf16[2048,384]{1,0:T(8,128)(2,1)}, u32[]{:S(2)}) copy-start(bf16[2048,384]{1,0:T(8,128)(2,1)} %param.15) | copy-start | bytes 4718596
  7.2 37.3 %all-gather.8.cloned.1.call-start = ((), (), s32[]{:S(2)}) async-start(), calls=%async_computation.3 | async-start | bytes 3932160 | tf_op jit(solution)/shard_map/all_gather | solution.py:108
  7.9 108.5 %all-gather.6.cloned.1.call-start = ((), (), s32[]{:S(2)}) async-start(), calls=%async_computation.2 | async-start | bytes 4718592 | tf_op jit(solution)/shard_map/all_gather | solution.py:106
  8.7 136.1 %all-gather.10.cloned.1.call-start = ((), (), s32[]{:S(2)}) async-start(), calls=%async_computation.4 | async-start | bytes 3932160 | tf_op jit(solution)/shard_map/all_gather | solution.py:109
  9.4 165.4 %all-gather.12.cloned.1.call-start = ((), (), s32[]{:S(2)}) async-start(), calls=%async_computation.5 | async-start | bytes 3932160 | tf_op jit(solution)/shard_map/all_gather | solution.py:110
  10.0 292.1 %reduce-scatter.3.cloned.1.call-start = ((), (), s32[]{:S(2)}) async-start(), calls=%async_computation.6 | async-start | bytes 4718592 | tf_op jit(solution)/shard_map/reduce_scatter | solution.py:121
  116.4 4.1 %copy-start.1 = (bf16[1024,2048]{1,0:T(8,128)(2,1)S(1)}, bf16[1024,2048]{1,0:T(8,128)(2,1)}, u32[]{:S(2)}) copy-start(bf16[1024,2048]{1,0:T(8,128)(2,1)} %all-gather.6.cloned.1.call-done) | copy-start | bytes 12582916
  116.4 4.7 %copy-start.3 = (bf16[4,2048,192]{1,2,0:T(8,128)(2,1)S(1)}, bf16[4,2048,192]{1,2,0:T(8,128)(2,1)}, u32[]{:S(2)}) copy-start(bf16[4,2048,192]{1,2,0:T(8,128)(2,1)} %all-gather.8.cloned.1.call-done) | copy-start | bytes 9437188
  192.2 9.9 %copy-start.6 = (f32[1024,192]{0,1:T(8,128)S(1)}, f32[1024,192]{0,1:T(8,128)}, u32[]{:S(2)}) copy-start(f32[1024,192]{0,1:T(8,128)} %fusion.8) | copy-start | bytes 2359300
  213.9 88.2 %copy-start.2 = (s32[512]{0:T(512)S(1)}, s32[512]{0:T(512)}, u32[]{:S(2)}) copy-start(s32[512]{0:T(512)} %param.17) | copy-start | bytes 6148
  213.9 115.7 %copy-start.5 = (bf16[512,384]{1,0:T(8,128)(2,1)S(1)}, bf16[512,384]{1,0:T(8,128)(2,1)}, u32[]{:S(2)}) copy-start(bf16[512,384]{1,0:T(8,128)(2,1)} %param.16) | copy-start | bytes 1179652
  214.0 111.9 %all-gather.14.cloned.1.call-start = ((), (), s32[]{:S(2)}) async-start(), calls=%async_computation.7 | async-start | bytes 2621440 | tf_op jit(solution)/shard_map/all_gather | solution.py:130
  302.1 95.1 %reduce-scatter.5.cloned.1.call-start = ((), (), s32[]{:S(2)}) async-start(), calls=%async_computation.8 | async-start | bytes 1769472 | tf_op jit(solution)/shard_map/reduce_scatter | solution.py:138
  325.9 3.7 copy-start.4
Sparse Core Ops, SparseCore 0:
  9.6 31.2 all-gather.7
  43.0 73.3 all-gather.5
  118.0 26.7 all-gather.9
  146.2 28.5 all-gather.11
  214.1 87.8 reduce-scatter.2
  303.5 22.3 all-gather.13
  332.4 64.8 reduce-scatter.4

commit v2 on v0

--- a/solution.py
+++ b/solution.py
@@ -1,8 +1,11 @@
+import functools
 import math
 
 import jax
 import jax.numpy as jnp
 from jax import lax
+from jax.experimental import pallas as pl
+from jax.experimental.pallas import tpu as pltpu
 from jax.sharding import PartitionSpec as P
 
 
@@ -22,7 +25,7 @@
     return (jax.nn.silu(gate_pre) * up_pre).astype(jnp.bfloat16)
 
 
-def body(tokens, expert_ids, gate_scores, w_gate, w_up, w_down, projector, student, target_mask):
+def routed_body(tokens, expert_ids, gate_scores, w_gate, w_up, w_down, projector, student, target_mask):
     tok_count = tokens.shape[0]
     model_width = tokens.shape[1]
     top_count = expert_ids.shape[1]
@@ -89,7 +92,436 @@
         picked = jnp.take(returned, position[:, column], axis=0)
         combined = combined + norm_gates[:, column : column + 1] * picked.astype(jnp.float32)
     teacher_out = combined.astype(jnp.bfloat16)
-    grad_scale = 1.0 / math.sqrt(tok_count * expert_axis * data_axis)
+    return finish(teacher_out, projector, student, target_mask)
+
+
+MESH = pl.DeviceIdType.MESH
+
+
+def over_rows(count, step, work):
+    def one(i, carry):
+        work(pl.ds(pl.multiple_of(i * step, step), step))
+        return carry
+
+    lax.fori_loop(0, count // step, one, 0)
+
+
+def fused_kernel(
+    expert_axis,
+    grad_scale,
+    tokens_ref,
+    ids_ref,
+    scores_ref,
+    gate_ref,
+    up_ref,
+    down_ref,
+    projector_ref,
+    student_ref,
+    mask_ref,
+    projected_ref,
+    grad_ref,
+    tok,
+    gate_up,
+    down,
+    acc,
+    pair_send,
+    pair_recv,
+    line_send,
+    line_recv,
+    teach,
+    error,
+    grad_acc,
+    gpair_send,
+    gpair_recv,
+    gline_send,
+    gline_recv,
+    tok_send_sem,
+    tok_recv_sem,
+    w_send_sem,
+    w_recv_sem,
+    pair_sem,
+    line_sem,
+    teach_send_sem,
+    teach_recv_sem,
+    gpair_sem,
+    gline_sem,
+):
+    rows, width = tokens_ref.shape
+    top_count = ids_ref.shape[1]
+    half = gate_ref.shape[2]
+    features = projector_ref.shape[1]
+    line = expert_axis // 2
+    e = lax.axis_index("expert")
+    d = lax.axis_index("dp")
+    z, y = e // 2, e % 2
+    x, c = d // 2, d % 2
+    peer = e + 1 - 2 * y
+    mate = d + 1 - 2 * c
+    cross = d + 2 - 4 * x
+    diagonal = cross + 1 - 2 * c
+    has_low, has_high = z > 0, z < line - 1
+
+    def remote(src, dst, send, recv, to_e, to_d):
+        return pltpu.make_async_remote_copy(
+            src_ref=src, dst_ref=dst, send_sem=send, recv_sem=recv,
+            device_id={"expert": to_e, "dp": to_d}, device_id_type=MESH,
+        )
+
+    barrier = pltpu.get_barrier_semaphore()
+
+    def greet(to_e, to_d):
+        pl.semaphore_signal(
+            barrier, inc=1, device_id={"expert": to_e, "dp": to_d}, device_id_type=MESH
+        )
+
+    greet(peer, d)
+    greet(e, mate)
+    greet(e, cross)
+
+    @pl.when(has_low)
+    def _():
+        greet(e - 2, d)
+
+    @pl.when(has_high)
+    def _():
+        greet(e + 2, d)
+
+    ends = jnp.where(z == 0, 1, 0) + jnp.where(z == line - 1, 1, 0)
+    pl.semaphore_wait(barrier, 5 - ends)
+
+    def tok_copy(row, way):
+        slot = 2 * row + y
+        to_e = (e + 2, e - 2, peer)[way]
+        return remote(
+            tok.at[slot], tok.at[slot], tok_send_sem.at[row, way], tok_recv_sem.at[slot], to_e, d
+        )
+
+    def tok_arrived(slot):
+        remote(
+            tok.at[slot], tok.at[slot], tok_send_sem.at[0, 0], tok_recv_sem.at[slot], peer, d
+        ).wait_recv()
+
+    scores = scores_ref[...]
+    norm = scores / jnp.sum(scores, axis=1, keepdims=True)
+    ids = ids_ref[...]
+    lane = lax.broadcasted_iota(jnp.int32, (rows, 128), 1)
+    named = lane % 64
+    dense = jnp.zeros((rows, 128), jnp.float32)
+    for j in range(top_count):
+        dense = dense + jnp.where(ids[:, j : j + 1] == named, norm[:, j : j + 1], 0.0)
+    coarse = dense.astype(jnp.bfloat16).astype(jnp.float32)
+    tok[e, :, width : width + 128] = jnp.where(lane < 64, coarse, dense - coarse).astype(jnp.bfloat16)
+    tok[e, :, 0:width] = tokens_ref[...]
+
+    @pl.when(has_high)
+    def _():
+        tok_copy(z, 0).start()
+
+    @pl.when(has_low)
+    def _():
+        tok_copy(z, 1).start()
+
+    tok_copy(z, 2).start()
+
+    def w_copy(piece, slab, way):
+        if piece < 2:
+            part = pl.ds(piece * (width // 2), width // 2)
+            ref = gate_up.at[slab, part]
+        else:
+            ref = down.at[slab]
+        return remote(
+            ref, ref, w_send_sem.at[piece, way], w_recv_sem.at[piece, slab], e,
+            (cross, mate, mate)[way],
+        )
+
+    for piece in range(2):
+        def join(part, piece=piece):
+            at = pl.ds(pl.multiple_of(piece * (width // 2) + part.start, 128), 128)
+            gate_up[d, at, 0:half] = gate_ref[0, at, :]
+            gate_up[d, at, half : 2 * half] = up_ref[0, at, :]
+
+        over_rows(width // 2, 128, join)
+        w_copy(piece, d, 0).start()
+        w_copy(piece, d, 1).start()
+    down[d] = down_ref[0]
+    w_copy(2, d, 0).start()
+    w_copy(2, d, 1).start()
+
+    def expert_on(row, chip, first):
+        base = 2 * chip
+        expert = 2 * e + chip
+        block = tok[pl.ds(2 * row, 2), :, 0:width].reshape(2 * rows, width)
+        hidden = []
+        for part in range(2):
+            both = jnp.dot(block, gate_up[base + part], preferred_element_type=jnp.float32)
+            pre, up = both[:, 0:half], both[:, half : 2 * half]
+            hidden.append((pre / (1.0 + jnp.exp(-pre)) * up).astype(jnp.bfloat16))
+        gates = tok[pl.ds(2 * row, 2), :, width : width + 128].astype(jnp.float32)
+        gates = gates.reshape(2 * rows, 128)
+        which = lax.broadcasted_iota(jnp.int32, (2 * rows, 128), 1) % 64
+        gate = jnp.sum(jnp.where(which == expert, gates, 0.0), axis=1, keepdims=True)
+        span = 512
+
+        def columns(i, carry):
+            at = pl.ds(pl.multiple_of(i * span, span), span)
+            out = jnp.dot(hidden[0], down[base, :, at], preferred_element_type=jnp.float32)
+            out += jnp.dot(hidden[1], down[base + 1, :, at], preferred_element_type=jnp.float32)
+            out = gate * out.astype(jnp.bfloat16).astype(jnp.float32)
+            out = out.reshape(2, rows, span)
+            if first:
+                acc[pl.ds(2 * row, 2), :, at] = out
+            else:
+                acc[pl.ds(2 * row, 2), :, at] += out
+            return carry
+
+        lax.fori_loop(0, width // span, columns, 0)
+
+    def near_first(j, carry):
+        reach, side = (j + 1) // 2, j % 2
+        row = z + reach * (1 - 2 * side)
+
+        @pl.when(jnp.logical_and(row >= 0, row < line))
+        def _():
+            @pl.when(row != z)
+            def _():
+                tok_arrived(2 * row + y)
+
+                @pl.when(jnp.logical_and(row < z, has_high))
+                def _():
+                    tok_copy(row, 0).start()
+
+                @pl.when(jnp.logical_and(row > z, has_low))
+                def _():
+                    tok_copy(row, 1).start()
+
+                tok_copy(row, 2).start()
+
+            @pl.when(row == z)
+            def _():
+                for piece in range(3):
+                    w_copy(piece, mate, 1).wait_recv()
+
+            tok_arrived(2 * row + 1 - y)
+            expert_on(row, x, True)
+
+        return carry
+
+    lax.fori_loop(0, 2 * line - 1, near_first, 0)
+    for piece in range(3):
+        w_copy(piece, cross, 1).wait_recv()
+        w_copy(piece, cross, 2).start()
+    for piece in range(3):
+        w_copy(piece, diagonal, 1).wait_recv()
+
+    def place(p):
+        k = line - 1 - p
+        return 2 * ((z // 2 + k // 2) % (line // 2)) + (z + k) % 2
+
+    def sum_over_experts(total, psend, precv, lsend, lrecv, psem, lsem, make, step, write):
+        count = total.shape[1]
+
+        def pair_copy(row):
+            return remote(psend.at[row], precv.at[row], psem.at[0, row], psem.at[1, row], peer, d)
+
+        def line_copy(way, row):
+            return remote(
+                lsend.at[way, row], lrecv.at[way, row], lsem.at[0, way, row],
+                lsem.at[1, way, row], e + 2 - 4 * way, d,
+            )
+
+        def produce(p, carry):
+            row = place(p)
+            make(row)
+
+            def narrow(part):
+                psend[row, part] = total[2 * row + 1 - y, part].astype(jnp.bfloat16)
+
+            over_rows(count, step, narrow)
+            pair_copy(row).start()
+            return carry
+
+        lax.fori_loop(0, line, produce, 0)
+
+        def pass_on(p, carry):
+            row = place(p)
+            own = 2 * row + y
+            pair_copy(row).wait_recv()
+
+            def add_pair(part):
+                total[own, part] += precv[row, part].astype(jnp.float32)
+
+            over_rows(count, step, add_pair)
+
+            for way, before, beyond in ((0, has_low, row >= z), (1, has_high, row <= z)):
+                @pl.when(jnp.logical_and(before, beyond))
+                def _():
+                    line_copy(way, row).wait_recv()
+
+                    def add_line(part):
+                        total[own, part] += lrecv[way, row, part].astype(jnp.float32)
+
+                    over_rows(count, step, add_line)
+
+            for way, further in ((0, row > z), (1, row < z)):
+                @pl.when(further)
+                def _():
+                    def narrow(part):
+                        lsend[way, row, part] = total[own, part].astype(jnp.bfloat16)
+
+                    over_rows(count, step, narrow)
+                    line_copy(way, row).start()
+
+            return carry
+
+        lax.fori_loop(0, line, pass_on, 0)
+
+        def finish_row(part):
+            write(part, total[e, part])
+
+        over_rows(count, step, finish_row)
+
+        def settle(row, carry):
+            pair_copy(row).wait_send()
+            for way, further in ((0, row > z), (1, row < z)):
+                @pl.when(further)
+                def _():
+                    line_copy(way, row).wait_send()
+            return carry
+
+        lax.fori_loop(0, line, settle, 0)
+
+    def write_teacher(part, value):
+        teach[d, part] = value.astype(jnp.bfloat16)
+
+    sum_over_experts(
+        acc, pair_send, pair_recv, line_send, line_recv, pair_sem, line_sem,
+        lambda row: expert_on(row, 1 - x, False), 32, write_teacher,
+    )
+
+    def teach_copy(block, way):
+        return remote(
+            teach.at[block], teach.at[block], teach_send_sem.at[way], teach_recv_sem.at[block], e,
+            (cross, mate, mate)[way],
+        )
+
+    def project(block):
+        at = pl.ds(pl.multiple_of(block * rows, rows), rows)
+        value = jnp.dot(teach[block], projector_ref[...], preferred_element_type=jnp.float32)
+        projected_ref[at, :] = value.astype(jnp.bfloat16)
+        gap = value - student_ref[at, :].astype(jnp.float32)
+        error[at, :] = (mask_ref[at, :].astype(jnp.float32) * gap).astype(jnp.bfloat16)
+
+    teach_copy(d, 0).start()
+    teach_copy(d, 1).start()
+    project(d)
+    teach_copy(mate, 1).wait_recv()
+    project(mate)
+    teach_copy(cross, 1).wait_recv()
+    teach_copy(cross, 2).start()
+    project(cross)
+    teach_copy(diagonal, 1).wait_recv()
+    project(diagonal)
+
+    share = grad_acc.shape[1]
+    blocks = teach.shape[0]
+
+    def grad_of(row):
+        def one(side, carry):
+            target = 2 * row + side
+            at = pl.ds(pl.multiple_of(target * share, share), share)
+            grad_acc[target] = lax.dot_general(
+                teach[:, :, at].reshape(blocks * rows, share), error[...],
+                (((0,), (0,)), ((), ())), preferred_element_type=jnp.float32,
+            )
+            return carry
+
+        lax.fori_loop(0, 2, one, 0)
+
+    def write_grad(part, value):
+        grad_ref[part, :] = value * grad_scale
+
+    sum_over_experts(
+        grad_acc, gpair_send, gpair_recv, gline_send, gline_recv, gpair_sem, gline_sem,
+        grad_of, 64, write_grad,
+    )
+
+    def settle(row, carry):
+        @pl.when(jnp.logical_and(row <= z, has_high))
+        def _():
+            tok_copy(row, 0).wait_send()
+
+        @pl.when(jnp.logical_and(row >= z, has_low))
+        def _():
+            tok_copy(row, 1).wait_send()
+
+        tok_copy(row, 2).wait_send()
+        return carry
+
+    lax.fori_loop(0, line, settle, 0)
+    for piece in range(3):
+        w_copy(piece, d, 0).wait_send()
+        w_copy(piece, d, 1).wait_send()
+        w_copy(piece, cross, 2).wait_send()
+    teach_copy(d, 0).wait_send()
+    teach_copy(d, 1).wait_send()
+    teach_copy(cross, 2).wait_send()
+
+
+def fused_body(tokens, expert_ids, gate_scores, w_gate, w_up, w_down, projector, student, target_mask):
+    rows, width = tokens.shape
+    expert_axis, data_axis = lax.axis_size("expert"), lax.axis_size("dp")
+    half, features = w_gate.shape[2], projector.shape[1]
+    line, share = expert_axis // 2, width // expert_axis
+    grad_scale = 1.0 / math.sqrt(rows * expert_axis * data_axis)
+    bf16, f32 = jnp.bfloat16, jnp.float32
+    dma = pltpu.SemaphoreType.DMA
+    vmem = pl.BlockSpec(memory_space=pltpu.VMEM)
+    return pl.pallas_call(
+        functools.partial(fused_kernel, expert_axis, grad_scale),
+        out_shape=(
+            jax.ShapeDtypeStruct(student.shape, bf16),
+            jax.ShapeDtypeStruct((share, features), f32),
+        ),
+        in_specs=[vmem] * 9,
+        out_specs=(vmem, vmem),
+        scratch_shapes=[
+            pltpu.VMEM((expert_axis, rows, width + 128), bf16),
+            pltpu.VMEM((data_axis, width, 2 * half), bf16),
+            pltpu.VMEM((data_axis, half, width), bf16),
+            pltpu.VMEM((expert_axis, rows, width), f32),
+            pltpu.VMEM((line, rows, width), bf16),
+            pltpu.VMEM((line, rows, width), bf16),
+            pltpu.VMEM((2, line, rows, width), bf16),
+            pltpu.VMEM((2, line, rows, width), bf16),
+            pltpu.VMEM((data_axis, rows, width), bf16),
+            pltpu.VMEM((data_axis * rows, features), bf16),
+            pltpu.VMEM((expert_axis, share, features), f32),
+            pltpu.VMEM((line, share, features), bf16),
+            pltpu.VMEM((line, share, features), bf16),
+            pltpu.VMEM((2, line, share, features), bf16),
+            pltpu.VMEM((2, line, share, features), bf16),
+            dma((line, 3)),
+            dma((expert_axis,)),
+            dma((3, 3)),
+            dma((3, data_axis)),
+            dma((2, line)),
+            dma((2, 2, line)),
+            dma((3,)),
+            dma((data_axis,)),
+            dma((2, line)),
+            dma((2, 2, line)),
+        ],
+        compiler_params=pltpu.CompilerParams(
+            collective_id=0, has_side_effects=True, vmem_limit_bytes=60 * 1024 * 1024
+        ),
+    )(
+        tokens, expert_ids, gate_scores, w_gate, w_up, w_down, projector, student,
+        target_mask.reshape(-1, 1),
+    )
+
+
+def finish(teacher_out, projector, student, target_mask):
+    grad_scale = 1.0 / math.sqrt(teacher_out.shape[0] * lax.axis_size("expert") * lax.axis_size("dp"))
     mask_rows = target_mask.astype(jnp.float32)
     portion = lax.all_gather(teacher_out, "dp", axis=0, tiled=True)
     proj_part = jnp.dot(portion, projector, preferred_element_type=jnp.float32)
@@ -98,18 +530,18 @@
     grad_term = lax.dot_general(
         portion, error_part, (((0,), (0,)), ((), ())), preferred_element_type=jnp.float32
     )
-    projected_all = proj_part
-    projected_all, grad_term = (projected_all, grad_term)
     grad_part = (
         lax.psum_scatter(
             grad_term.astype(jnp.bfloat16), "expert", scatter_dimension=0, tiled=True
         ).astype(jnp.float32)
         * grad_scale
     )
-    return (projected_all.astype(jnp.bfloat16), grad_part)
+    return (proj_part.astype(jnp.bfloat16), grad_part)
 
 
 def solution(mesh):
+    fits = mesh.shape["expert"] == 8 and mesh.shape["dp"] == 4
+    body = fused_body if fits else routed_body
     return jax.shard_map(
         body,
         mesh=mesh,

time: 665 us -> 200 us (0.30)
  blocking collectives: 287 us -> 0 us
  waiting for transfers between devices: 226 us -> 0 us
  Pallas kernels: 0 us -> 188 us
  local copies, waits for them, and re-layouts: 74.1 us -> 11.5 us
  matrix products: 39.4 us -> 0 us
  between operations: 14.3 us -> 0.65 us
  starting transfers between devices: 12 us -> 0 us
  other arithmetic: 11 us -> 0 us
    all_to_all x2 -> x0, blocking collectives: 287 us -> none  [the longest x1 145 us: body(): lax.all_to_all(send_rows, 'expert', split_axis=0, concat_axis=0, tiled=True)]
    pallas_call x0 -> x1, Pallas kernels: none -> 188 us  [fused_body(): pl.pallas_call(functools.partial(fused_kernel, expert_axis, grad_scale),...]
    all_to_all x2 -> x0, waiting for transfers between devices: 140 us -> none  [the longest x1 70.3 us: body(): lax.all_to_all(lax.all_to_all(expert_out.reshape(expert_axis, data_axis,...]
    reduce_scatter x1 -> x0, waiting for transfers between devices: 65.1 us -> none  [body(): lax.psum_scatter(grad_term.astype(jnp.bfloat16), 'expert', scatter_dimens...]
    gather x9 -> x0, local copies, waits for them, and re-layouts: 51.7 us -> none  [the longest x8 44.6 us: body(): picked = jnp.take(returned, position[:, column], axis=0)]
    dot_general x6 -> x0, matrix products: 39.4 us -> none  [the longest x1 13.4 us: body(): jnp.dot(hidden_other, down_other, preferred_element_type=jnp.float32)]
    all_gather x1 -> x0, waiting for transfers between devices: 20.7 us -> none  [body(): portion = lax.all_gather(teacher_out, 'dp', axis=0, tiled=True)]
    all_to_all x4 -> x0, local copies, waits for them, and re-layouts: 16.4 us -> none  [the longest x1 6.58 us: body(): lax.all_to_all(lax.all_to_all(expert_out.reshape(expert_axis, data_axis,...]
  transfers between devices with their start and end apart: 7 -> 0, of which waited for: 4 -> 0; matrix products, arithmetic and copies ran while one was open for 3% -> 0% of each run, Pallas kernels for 0% -> 0%
where the time goes in v2:
time: 200 us
  Pallas kernels  188 us (94%)
  local copies, waits for them, and re-layouts  11.5 us (6%)
    pallas_call x1, Pallas kernels, fused_body(): pl.pallas_call(functools.partial(fused_kernel, expert_axis, grad_scale),...  188 us
    unnamed x8, local copies, waits for them, and re-layouts  9.95 us

profile of v2, /device:TPU:0, one launch (start us, length us, event | category | flops | bytes accessed | tf_op | source)
XLA Modules:
  0.0 199.7 jit_solution(1435024362398427404)
XLA Ops:
  0.6 0.0 copy-start
  0.6 1.5 copy.15.ids_ref
  2.1 1.4 copy.16.scores_ref
  3.5 1.5 copy.19.mask_ref
  5.1 2.2 %copy.17.gate_ref = bf16[1,2048,192]{2,1,0:T(8,128)(2,1)} copy(bf16[1,2048,192]{1,2,0:T(8,128)(2,1)} %param.12) | data formatting | bytes 1572864 | tf_op args[3]
  7.3 0.0 copy-done
  7.3 1.3 copy.18.up_ref
  8.6 187.5 %shard_map.104 = (bf16[512,384]{1,0:T(8,128)(2,1)}, f32[256,384]{1,0:T(8,128)}) custom-call(bf16[128,2048]{1,0:T(8,128)(2,1)} %tokens_ref.1, s32[128,8]{1,0:T(8,128)} %copy.15.ids_ref, f32[128,8]{1,0:T(8,128)} %copy.16.scores_ref, bf16[1,2048,192]{2,1,0:T(8,128)(2,1)} %copy.17.gate_ref, bf16[1,2048,192]{2,1,0:T(8,128)(2,1)} %copy.18.up_ref, ...), custom_call_target="tpu_custom_call" | custom-call | tf_op jit(solution)/shard_map/pallas_call | solution.py:479
  196.1 1.8 copy.22
  197.9 1.8 copy.23
Async XLA Ops:
  0.6 6.6 %copy-start = (bf16[1,2048,192]{1,2,0:T(8,128)(2,1)S(1)}, bf16[1,2048,192]{1,2,0:T(8,128)(2,1)}, u32[]{:S(2)}) copy-start(bf16[1,2048,192]{1,2,0:T(8,128)(2,1)} %param.13) | copy-start | bytes 2359300

commit v3 on v2

--- a/solution.py
+++ b/solution.py
@@ -147,8 +147,8 @@
     gline_sem,
 ):
     rows, width = tokens_ref.shape
-    top_count = ids_ref.shape[1]
-    half = gate_ref.shape[2]
+    top_count = ids_ref.shape[0]
+    half = gate_ref.shape[1]
     features = projector_ref.shape[1]
     line = expert_axis // 2
     e = lax.axis_index("expert")
@@ -202,13 +202,14 @@
         ).wait_recv()
 
     scores = scores_ref[...]
-    norm = scores / jnp.sum(scores, axis=1, keepdims=True)
+    norm = scores / jnp.sum(scores, axis=0, keepdims=True)
     ids = ids_ref[...]
+    named = lax.broadcasted_iota(jnp.int32, (128, rows), 0) % 64
+    dense = jnp.zeros((128, rows), jnp.float32)
+    for j in range(top_count):
+        dense = dense + jnp.where(ids[j : j + 1, :] == named, norm[j : j + 1, :], 0.0)
+    dense = dense.T
     lane = lax.broadcasted_iota(jnp.int32, (rows, 128), 1)
-    named = lane % 64
-    dense = jnp.zeros((rows, 128), jnp.float32)
-    for j in range(top_count):
-        dense = dense + jnp.where(ids[:, j : j + 1] == named, norm[:, j : j + 1], 0.0)
     coarse = dense.astype(jnp.bfloat16).astype(jnp.float32)
     tok[e, :, width : width + 128] = jnp.where(lane < 64, coarse, dense - coarse).astype(jnp.bfloat16)
     tok[e, :, 0:width] = tokens_ref[...]
@@ -225,8 +226,7 @@
 
     def w_copy(piece, slab, way):
         if piece < 2:
-            part = pl.ds(piece * (width // 2), width // 2)
-            ref = gate_up.at[slab, part]
+            ref = gate_up.at[slab, pl.ds(piece * half, half)]
         else:
             ref = down.at[slab]
         return remote(
@@ -234,15 +234,12 @@
             (cross, mate, mate)[way],
         )
 
-    for piece in range(2):
-        def join(part, piece=piece):
-            at = pl.ds(pl.multiple_of(piece * (width // 2) + part.start, 128), 128)
-            gate_up[d, at, 0:half] = gate_ref[0, at, :]
-            gate_up[d, at, half : 2 * half] = up_ref[0, at, :]
-
-        over_rows(width // 2, 128, join)
-        w_copy(piece, d, 0).start()
-        w_copy(piece, d, 1).start()
+    gate_up[d, 0:half] = gate_ref[0]
+    w_copy(0, d, 0).start()
+    w_copy(0, d, 1).start()
+    gate_up[d, half : 2 * half] = up_ref[0]
+    w_copy(1, d, 0).start()
+    w_copy(1, d, 1).start()
     down[d] = down_ref[0]
     w_copy(2, d, 0).start()
     w_copy(2, d, 1).start()
@@ -253,7 +250,10 @@
         block = tok[pl.ds(2 * row, 2), :, 0:width].reshape(2 * rows, width)
         hidden = []
         for part in range(2):
-            both = jnp.dot(block, gate_up[base + part], preferred_element_type=jnp.float32)
+            both = lax.dot_general(
+                block, gate_up[base + part], (((1,), (1,)), ((), ())),
+                preferred_element_type=jnp.float32,
+            )
             pre, up = both[:, 0:half], both[:, half : 2 * half]
             hidden.append((pre / (1.0 + jnp.exp(-pre)) * up).astype(jnp.bfloat16))
         gates = tok[pl.ds(2 * row, 2), :, width : width + 128].astype(jnp.float32)
@@ -276,37 +276,41 @@
 
         lax.fori_loop(0, width // span, columns, 0)
 
-    def near_first(j, carry):
-        reach, side = (j + 1) // 2, j % 2
-        row = z + reach * (1 - 2 * side)
-
-        @pl.when(jnp.logical_and(row >= 0, row < line))
-        def _():
-            @pl.when(row != z)
+    def near_first(reach, carry):
+        for side in (-1, 1):
+            row = z + side * (reach + 1)
+
+            @pl.when(jnp.logical_and(row >= 0, row < line))
             def _():
                 tok_arrived(2 * row + y)
 
-                @pl.when(jnp.logical_and(row < z, has_high))
+                @pl.when(has_high if side < 0 else has_low)
                 def _():
-                    tok_copy(row, 0).start()
-
-                @pl.when(jnp.logical_and(row > z, has_low))
-                def _():
-                    tok_copy(row, 1).start()
+                    tok_copy(row, (1 + side) // 2).start()
 
                 tok_copy(row, 2).start()
 
-            @pl.when(row == z)
+        @pl.when(reach == 0)
+        def _():
+            for piece in range(3):
+                w_copy(piece, mate, 1).wait_recv()
+
+        def one_side(side, inner):
+            row = z + reach * (2 * side - 1)
+
+            @pl.when(
+                jnp.logical_and(jnp.logical_and(row >= 0, row < line), reach + side > 0)
+            )
             def _():
-                for piece in range(3):
-                    w_copy(piece, mate, 1).wait_recv()
-
-            tok_arrived(2 * row + 1 - y)
-            expert_on(row, x, True)
-
+                tok_arrived(2 * row + 1 - y)
+                expert_on(row, x, True)
+
+            return inner
+
+        lax.fori_loop(0, 2, one_side, 0)
         return carry
 
-    lax.fori_loop(0, 2 * line - 1, near_first, 0)
+    lax.fori_loop(0, line, near_first, 0)
     for piece in range(3):
         w_copy(piece, cross, 1).wait_recv()
         w_copy(piece, cross, 2).start()
@@ -409,7 +413,8 @@
         value = jnp.dot(teach[block], projector_ref[...], preferred_element_type=jnp.float32)
         projected_ref[at, :] = value.astype(jnp.bfloat16)
         gap = value - student_ref[at, :].astype(jnp.float32)
-        error[at, :] = (mask_ref[at, :].astype(jnp.float32) * gap).astype(jnp.bfloat16)
+        mask = jnp.broadcast_to(mask_ref[:, at].astype(jnp.float32), (128, rows)).T[:, 0:1]
+        error[at, :] = (mask * gap).astype(jnp.bfloat16)
 
     teach_copy(d, 0).start()
     teach_copy(d, 1).start()
@@ -486,7 +491,7 @@
         out_specs=(vmem, vmem),
         scratch_shapes=[
             pltpu.VMEM((expert_axis, rows, width + 128), bf16),
-            pltpu.VMEM((data_axis, width, 2 * half), bf16),
+            pltpu.VMEM((data_axis, 2 * half, width), bf16),
             pltpu.VMEM((data_axis, half, width), bf16),
             pltpu.VMEM((expert_axis, rows, width), f32),
             pltpu.VMEM((line, rows, width), bf16),
@@ -515,8 +520,8 @@
             collective_id=0, has_side_effects=True, vmem_limit_bytes=60 * 1024 * 1024
         ),
     )(
-        tokens, expert_ids, gate_scores, w_gate, w_up, w_down, projector, student,
-        target_mask.reshape(-1, 1),
+        tokens, expert_ids.T, gate_scores.T, jnp.swapaxes(w_gate, 1, 2),
+        jnp.swapaxes(w_up, 1, 2), w_down, projector, student, target_mask.reshape(1, -1),
     )
 
 

time: 200 us -> 183 us (0.915)
  Pallas kernels: 188 us -> 179 us
  local copies, waits for them, and re-layouts: 11.5 us -> 3.55 us
    pallas_call x1, Pallas kernels: 188 us -> 179 us  [fused_body(): pl.pallas_call(functools.partial(fused_kernel, expert_axis, grad_scale),...]
    unnamed x8 -> x2, local copies, waits for them, and re-layouts: 9.95 us -> 3.55 us
where the time goes in v3:
time: 183 us
  Pallas kernels  179 us (98%)
  local copies, waits for them, and re-layouts  3.55 us (2%)
    pallas_call x1, Pallas kernels, fused_body(): pl.pallas_call(functools.partial(fused_kernel, expert_axis, grad_scale),...  179 us

profile of v3, /device:TPU:0, one launch (start us, length us, event | category | flops | bytes accessed | tf_op | source)
XLA Modules:
  0.0 182.8 jit_solution(16925211609331604900)
XLA Ops:
  0.6 178.6 %shard_map.104 = (bf16[512,384]{1,0:T(8,128)(2,1)}, f32[256,384]{1,0:T(8,128)}) custom-call(bf16[128,2048]{1,0:T(8,128)(2,1)} %tokens_ref.1, s32[8,128]{1,0:T(8,128)} %bitcast.7, f32[8,128]{1,0:T(8,128)} %bitcast.8, bf16[1,192,2048]{2,1,0:T(8,128)(2,1)} %bitcast.5, bf16[1,192,2048]{2,1,0:T(8,128)(2,1)} %bitcast.6, bf16[1,192,2048]{2,1,0:T(8,128)(2,1)} %down_ref.1, ...), custom_call_target="tpu_custom_call" | custom-call | tf_op jit(solution)/shard_map/pallas_call | solution.py:484
  179.2 1.8 copy.13
  181.0 1.8 copy.14

commit v4 on v3

--- a/solution.py
+++ b/solution.py
@@ -96,6 +96,8 @@
 
 
 MESH = pl.DeviceIdType.MESH
+SUM_PARTS = 4
+GRAD_PARTS = 2
 
 
 def over_rows(count, step, work):
@@ -321,85 +323,105 @@
         k = line - 1 - p
         return 2 * ((z // 2 + k // 2) % (line // 2)) + (z + k) % 2
 
-    def sum_over_experts(total, psend, precv, lsend, lrecv, psem, lsem, make, step, write):
-        count = total.shape[1]
-
-        def pair_copy(row):
-            return remote(psend.at[row], precv.at[row], psem.at[0, row], psem.at[1, row], peer, d)
-
-        def line_copy(way, row):
+    def sum_over_experts(total, psend, precv, lsend, lrecv, psem, lsem, make, parts, step, write):
+        count = total.shape[1] // parts
+
+        def piece_at(part):
+            return pl.ds(pl.multiple_of(part * count, count), count)
+
+        def pair_copy(row, part):
+            at = piece_at(part)
             return remote(
-                lsend.at[way, row], lrecv.at[way, row], lsem.at[0, way, row],
-                lsem.at[1, way, row], e + 2 - 4 * way, d,
+                psend.at[row, at], precv.at[row, at], psem.at[0, row, part],
+                psem.at[1, row, part], peer, d,
             )
+
+        def line_copy(way, row, part):
+            at = piece_at(part)
+            return remote(
+                lsend.at[way, row, at], lrecv.at[way, row, at], lsem.at[0, way, row, part],
+                lsem.at[1, way, row, part], e + 2 - 4 * way, d,
+            )
+
+        def over_piece(part, work):
+            def one(i, carry):
+                work(pl.ds(pl.multiple_of(part * count + i * step, step), step))
+                return carry
+
+            lax.fori_loop(0, count // step, one, 0)
 
         def produce(p, carry):
             row = place(p)
             make(row)
 
-            def narrow(part):
-                psend[row, part] = total[2 * row + 1 - y, part].astype(jnp.bfloat16)
-
-            over_rows(count, step, narrow)
-            pair_copy(row).start()
+            def narrow(at):
+                psend[row, at] = total[2 * row + 1 - y, at].astype(jnp.bfloat16)
+
+            def send(part, inner):
+                over_piece(part, narrow)
+                pair_copy(row, part).start()
+                return inner
+
+            lax.fori_loop(0, parts, send, 0)
             return carry
 
         lax.fori_loop(0, line, produce, 0)
 
-        def pass_on(p, carry):
-            row = place(p)
+        def pass_on(q, carry):
+            row, part = place(q // parts), q % parts
             own = 2 * row + y
-            pair_copy(row).wait_recv()
-
-            def add_pair(part):
-                total[own, part] += precv[row, part].astype(jnp.float32)
-
-            over_rows(count, step, add_pair)
+            pair_copy(row, part).wait_recv()
+
+            def add_pair(at):
+                total[own, at] += precv[row, at].astype(jnp.float32)
+
+            over_piece(part, add_pair)
 
             for way, before, beyond in ((0, has_low, row >= z), (1, has_high, row <= z)):
                 @pl.when(jnp.logical_and(before, beyond))
                 def _():
-                    line_copy(way, row).wait_recv()
-
-                    def add_line(part):
-                        total[own, part] += lrecv[way, row, part].astype(jnp.float32)
-
-                    over_rows(count, step, add_line)
+                    line_copy(way, row, part).wait_recv()
+
+                    def add_line(at):
+                        total[own, at] += lrecv[way, row, at].astype(jnp.float32)
+
+                    over_piece(part, add_line)
 
             for way, further in ((0, row > z), (1, row < z)):
                 @pl.when(further)
                 def _():
-                    def narrow(part):
-                        lsend[way, row, part] = total[own, part].astype(jnp.bfloat16)
-
-                    over_rows(count, step, narrow)
-                    line_copy(way, row).start()
+                    def narrow(at):
+                        lsend[way, row, at] = total[own, at].astype(jnp.bfloat16)
+
+                    over_piece(part, narrow)
+                    line_copy(way, row, part).start()
 
             return carry
 
-        lax.fori_loop(0, line, pass_on, 0)
-
-        def finish_row(part):
-            write(part, total[e, part])
-
-        over_rows(count, step, finish_row)
-
-        def settle(row, carry):
-            pair_copy(row).wait_send()
+        lax.fori_loop(0, line * parts, pass_on, 0)
+
+        def finish_row(at):
+            write(at, total[e, at])
+
+        over_rows(total.shape[1], step, finish_row)
+
+        def settle(q, carry):
+            row, part = q // parts, q % parts
+            pair_copy(row, part).wait_send()
             for way, further in ((0, row > z), (1, row < z)):
                 @pl.when(further)
                 def _():
-                    line_copy(way, row).wait_send()
+                    line_copy(way, row, part).wait_send()
             return carry
 
-        lax.fori_loop(0, line, settle, 0)
+        lax.fori_loop(0, line * parts, settle, 0)
 
     def write_teacher(part, value):
         teach[d, part] = value.astype(jnp.bfloat16)
 
     sum_over_experts(
         acc, pair_send, pair_recv, line_send, line_recv, pair_sem, line_sem,
-        lambda row: expert_on(row, 1 - x, False), 32, write_teacher,
+        lambda row: expert_on(row, 1 - x, False), SUM_PARTS, 16, write_teacher,
     )
 
     def teach_copy(block, way):
@@ -447,7 +469,7 @@
 
     sum_over_experts(
         grad_acc, gpair_send, gpair_recv, gline_send, gline_recv, gpair_sem, gline_sem,
-        grad_of, 64, write_grad,
+        grad_of, GRAD_PARTS, 64, write_grad,
     )
 
     def settle(row, carry):
@@ -509,12 +531,12 @@
             dma((expert_axis,)),
             dma((3, 3)),
             dma((3, data_axis)),
-            dma((2, line)),
-            dma((2, 2, line)),
+            dma((2, line, SUM_PARTS)),
+            dma((2, 2, line, SUM_PARTS)),
             dma((3,)),
             dma((data_axis,)),
-            dma((2, line)),
-            dma((2, 2, line)),
+            dma((2, line, GRAD_PARTS)),
+            dma((2, 2, line, GRAD_PARTS)),
         ],
         compiler_params=pltpu.CompilerParams(
             collective_id=0, has_side_effects=True, vmem_limit_bytes=60 * 1024 * 1024

time: 183 us -> 165 us (0.902)
  Pallas kernels: 179 us -> 160 us
    pallas_call x1, Pallas kernels: 179 us -> 160 us  [fused_body(): pl.pallas_call(functools.partial(fused_kernel, expert_axis, grad_scale),...]
where the time goes in v4:
time: 165 us; the launch traced here: 164 us
  Pallas kernels  160 us (97%)
  local copies, waits for them, and re-layouts  3.55 us (2%)
    pallas_call x1, Pallas kernels, fused_body(): pl.pallas_call(functools.partial(fused_kernel, expert_axis, grad_scale),...  160 us
    unnamed x2, local copies, waits for them, and re-layouts  3.55 us

profile of v4, /device:TPU:0, one launch (start us, length us, event | category | flops | bytes accessed | tf_op | source)
XLA Modules:
  0.0 164.0 jit_solution(10339219454823332383)
XLA Ops:
  0.6 159.8 %shard_map.104 = (bf16[512,384]{1,0:T(8,128)(2,1)}, f32[256,384]{1,0:T(8,128)}) custom-call(bf16[128,2048]{1,0:T(8,128)(2,1)} %tokens_ref.1, s32[8,128]{1,0:T(8,128)} %bitcast.7, f32[8,128]{1,0:T(8,128)} %bitcast.8, bf16[1,192,2048]{2,1,0:T(8,128)(2,1)} %bitcast.5, bf16[1,192,2048]{2,1,0:T(8,128)(2,1)} %bitcast.6, bf16[1,192,2048]{2,1,0:T(8,128)(2,1)} %down_ref.1, ...), custom_call_target="tpu_custom_call" | custom-call | tf_op jit(solution)/shard_map/pallas_call | solution.py:506
  160.5 1.8 %copy.13 = bf16[512,384]{1,0:T(8,128)(2,1)} copy(bf16[512,384]{1,0:T(8,128)(2,1)} %get-tuple-element.4) | data formatting | bytes 786432
  162.2 1.8 %copy.14 = f32[256,384]{1,0:T(8,128)} copy(f32[256,384]{1,0:T(8,128)} %get-tuple-element.5) | data formatting | bytes 786432
